TPU v7x, 32 devices: a whole 2x2x4 slice. The times are simulated.
32 devices in a mesh: grp: 4 (over y, x), row: 8 (over z, core).
Axes of the slice: x: 2, y: 2, z: 4, core: 2. Of those that a mesh axis runs over, the one named last changes fastest.
Arguments:
- b_tensor: bfloat16 [9984, 8, 768], P(None, 'grp', 'row'), may hold values from -0.21875 to 0.21875
- aux_counts: int32 [4], replicated, may hold values from 1 to 2, as said below
Outputs:
- exchange_matrix: float32 [9984, 9984], P('row', 'grp')
Inputs may be any that keep to these rules, and one draw needn't show every extreme that they name: `aux_counts`: some group has all 2 slots live.
All inputs are finite; a program needn't handle non-finite values.
Results may differ from a plain program's by a relative error of at most 0.0003.
Values may be sent and summed in bfloat16 or wider, within the bound.
A program may use at most 256 MiB of HBM per device.

v0:
```python
import jax
import jax.numpy as jnp
from jax import lax
from jax.sharding import PartitionSpec as P


def shifted(block, axis, distance):
    devices = range(lax.axis_size(axis))
    route = [((i - distance) % len(devices), i) for i in devices]
    return lax.ppermute(block, axis, route)


def shards(b_tensor, aux_counts):
    row_count = lax.axis_size("row")
    row_rank = lax.axis_index("row")
    group_index = lax.axis_index("grp")
    slot_count = b_tensor.shape[1]
    live_count = lax.dynamic_index_in_dim(aux_counts, group_index, 0, keepdims=False)
    live_mask = (jnp.arange(slot_count) < live_count).astype(jnp.bfloat16)
    masked = b_tensor * live_mask[None, :, None]
    regrouped = lax.all_to_all(masked, "row", split_axis=0, concat_axis=2, tiled=True)
    block_size = regrouped.shape[0]
    own_rows = regrouped.reshape(block_size, -1)

    def tile_with(visitor):
        return lax.dot_general(
            own_rows, visitor, (((1,), (1,)), ((), ())), preferred_element_type=jnp.float32
        )

    upper_part = jnp.zeros((block_size, row_count, block_size), jnp.float32)
    upper_part = lax.dynamic_update_index_in_dim(upper_part, tile_with(own_rows), row_rank, 1)

    def advance(cycle_step, state_tuple):
        visiting, upper_acc = state_tuple
        visiting = shifted(visiting, "row", -1)
        target = (row_rank + cycle_step) % row_count
        upper_acc = lax.dynamic_update_index_in_dim(upper_acc, tile_with(visiting), target, 1)
        return (visiting, upper_acc)

    visiting, upper_part = lax.fori_loop(1, row_count, advance, (own_rows, upper_part))
    partial_value = upper_part.reshape(block_size, row_count * block_size)
    return lax.psum_scatter(partial_value, "grp", scatter_dimension=1, tiled=True)


def solution(mesh):
    return jax.shard_map(
        shards,
        mesh=mesh,
        in_specs=(P(None, "grp", "row"), P()),
        out_specs=P("row", "grp"),
        check_vma=False,
    )
```

profile of v0, /device:TPU:2, one launch (start us, length us, event | category | flops | bytes accessed | tf_op | source)
XLA Modules:
  0.0 1108.7 jit_solution(14453963095908325986)
XLA Ops:
  6.5 1.2 dynamic_slice.4
  7.8 0.6 compare_convert_fusion
  8.4 4.2 broadcast_multiply_fusion
  12.7 11.6 %copy.16 = bf16[9984,2,96]{2,1,0:T(2,128)(2,1)} copy(bf16[9984,2,96]{0,2,1:T(8,128)(2,1)} %broadcast_multiply_fusion) | data formatting | bytes 7667712 | tf_op jit(solution)/shard_map/mul | solution.py:20
  24.3 4.9 all-to-all-start
  29.2 0.0 reduce-scatter.4.cloned.1.call-start
  29.2 113.7 %all-to-all-done = bf16[9984,2,96]{2,1,0:T(2,128)(2,1)} async-done(((bf16[9984,2,96]{2,1,0:T(2,128)(2,1)}), bf16[9984,2,96]{2,1,0:T(2,128)(2,1)}, u32[]{:S(2)}, u32[]{:S(2)}) %all-to-all-start) | async-done | bytes 3833888 | tf_op jit(solution)/shard_map/all_to_all | solution.py:21
  142.9 11.4 %copy.18 = bf16[8,1248,2,96]{1,3,0,2:T(8,128)(2,1)} copy(bf16[8,1248,2,96]{3,2,1,0:T(2,128)(2,1)} %bitcast.2) | data formatting | bytes 7667712 | tf_op jit(solution)/shard_map/all_to_all | solution.py:21
  154.4 6.2 copy.19
  160.6 4.2 copy.32
  164.8 0.0 copy-start
  164.8 16.9 %broadcast_in_dim.18 = f32[1248,8,1248]{2,0,1:T(8,128)} broadcast(f32[]{:T(128)} %constant.68.clone.1), dimensions={} | broadcast | bytes 49840132 | tf_op jit(solution)/shard_map/broadcast_in_dim | solution.py:30
  181.7 0.0 copy-done
  181.7 7.2 fusion.1
  189.0 413.9 %while.17 = (s32[]{:T(128)}, bf16[1248,1536]{1,0:T(8,128)(2,1)}, f32[1248,8,1248]{2,0,1:T(8,128)}, bf16[1248,1536]{1,0:T(8,128)(2,1)}, s32[]{:T(128)}, /*index=5*/s32[]{:T(128)}, s32[]{:T(128)}, s32[]{:T(128)}, s32[]{:T(128)}) while((s32[]{:T(128)}, bf16[1248,1536]{1,0:T(8,128)(2,1)}, f32[1248,8,1248]{2,0,1:T(8,128)}, ...), condition=%wide.region_1.2_spmd, body=%wide.region_0.1_spmd.sunk | while | flops 4784652288 | bytes 52396344 | solution.py:40
  189.0 0.9 collective-permute-start
  189.9 0.0 copy-start.1
  189.9 42.5 %collective-permute-done = bf16[1248,1536]{1,0:T(8,128)(2,1)} collective-permute-done((bf16[1248,1536]{1,0:T(8,128)(2,1)}, bf16[1248,1536]{1,0:T(8,128)(2,1)}, u32[]{:S(2)}, u32[]{:S(2)}) %collective-permute-start) | collective-permute-done | bytes 3833888 | tf_op jit(solution)/shard_map/while/body/eval_jaxpr/ppermute | solution.py:10
  232.3 4.2 copy.38
  236.6 0.0 copy-done.1
  236.6 9.2 fusion.10
  245.7 3.6 collective-permute-start
  249.4 0.0 copy-start.1
  249.4 42.5 %collective-permute-done = bf16[1248,1536]{1,0:T(8,128)(2,1)} collective-permute-done((bf16[1248,1536]{1,0:T(8,128)(2,1)}, bf16[1248,1536]{1,0:T(8,128)(2,1)}, u32[]{:S(2)}, u32[]{:S(2)}) %collective-permute-start) | collective-permute-done | bytes 3833888 | tf_op jit(solution)/shard_map/while/body/eval_jaxpr/ppermute | solution.py:10
  291.8 4.2 copy.38
  296.0 0.0 copy-done.1
  296.0 9.1 fusion.10
  305.2 3.8 collective-permute-start
  308.9 0.0 copy-start.1
  308.9 42.5 %collective-permute-done = bf16[1248,1536]{1,0:T(8,128)(2,1)} collective-permute-done((bf16[1248,1536]{1,0:T(8,128)(2,1)}, bf16[1248,1536]{1,0:T(8,128)(2,1)}, u32[]{:S(2)}, u32[]{:S(2)}) %collective-permute-start) | collective-permute-done | bytes 3833888 | tf_op jit(solution)/shard_map/while/body/eval_jaxpr/ppermute | solution.py:10
  351.4 4.2 copy.38
  355.6 0.0 copy-done.1
  355.6 9.2 fusion.10
  364.8 3.7 collective-permute-start
  368.4 0.0 copy-start.1
  368.4 42.5 %collective-permute-done = bf16[1248,1536]{1,0:T(8,128)(2,1)} collective-permute-done((bf16[1248,1536]{1,0:T(8,128)(2,1)}, bf16[1248,1536]{1,0:T(8,128)(2,1)}, u32[]{:S(2)}, u32[]{:S(2)}) %collective-permute-start) | collective-permute-done | bytes 3833888 | tf_op jit(solution)/shard_map/while/body/eval_jaxpr/ppermute | solution.py:10
  410.9 4.2 copy.38
  415.1 0.0 copy-done.1
  415.1 9.2 fusion.10
  424.3 3.7 collective-permute-start
  428.0 0.0 copy-start.1
  428.0 42.5 %collective-permute-done = bf16[1248,1536]{1,0:T(8,128)(2,1)} collective-permute-done((bf16[1248,1536]{1,0:T(8,128)(2,1)}, bf16[1248,1536]{1,0:T(8,128)(2,1)}, u32[]{:S(2)}, u32[]{:S(2)}) %collective-permute-start) | collective-permute-done | bytes 3833888 | tf_op jit(solution)/shard_map/while/body/eval_jaxpr/ppermute | solution.py:10
  470.5 4.2 copy.38
  474.7 0.0 copy-done.1
  474.7 9.2 fusion.10
  483.9 3.7 collective-permute-start
  487.5 0.0 copy-start.1
  487.5 42.5 %collective-permute-done = bf16[1248,1536]{1,0:T(8,128)(2,1)} collective-permute-done((bf16[1248,1536]{1,0:T(8,128)(2,1)}, bf16[1248,1536]{1,0:T(8,128)(2,1)}, u32[]{:S(2)}, u32[]{:S(2)}) %collective-permute-start) | collective-permute-done | bytes 3833888 | tf_op jit(solution)/shard_map/while/body/eval_jaxpr/ppermute | solution.py:10
  530.0 4.2 copy.38
  534.2 0.0 copy-done.1
  534.2 9.1 fusion.10
  543.3 3.8 collective-permute-start
  547.1 0.0 copy-start.1
  547.1 42.5 %collective-permute-done = bf16[1248,1536]{1,0:T(8,128)(2,1)} collective-permute-done((bf16[1248,1536]{1,0:T(8,128)(2,1)}, bf16[1248,1536]{1,0:T(8,128)(2,1)}, u32[]{:S(2)}, u32[]{:S(2)}) %collective-permute-start) | collective-permute-done | bytes 3833888 | tf_op jit(solution)/shard_map/while/body/eval_jaxpr/ppermute | solution.py:10
  589.6 4.2 copy.38
  593.8 0.0 copy-done.1
  593.8 9.1 fusion.10
  602.9 53.4 %copy.27 = f32[1248,8,1248]{0,2,1:T(8,128)} copy(f32[1248,8,1248]{2,0,1:T(8,128)} %get-tuple-element.138) | data formatting | bytes 99680256
  656.3 0.0 reduce-scatter.4.cloned.1.call-update
  656.3 431.9 %reduce-scatter.4.cloned.1.call-done = f32[2496,1248]{1,0:T(8,128)} async-done(((f32[9984,1248]{1,0:T(8,128)}), f32[2496,1248]{1,0:T(8,128)}) %reduce-scatter.4.cloned.1.call-update) | async-done | bytes 12460048
  1088.2 13.7 %copy.26 = f32[1248,2496]{1,0:T(8,128)} copy(f32[1248,2496]{0,1:T(8,128)} %bitcast.33) | data formatting | bytes 24920064
Async XLA Ops:
  24.3 118.7 %all-to-all-start = ((bf16[9984,2,96]{2,1,0:T(2,128)(2,1)}), bf16[9984,2,96]{2,1,0:T(2,128)(2,1)}, u32[]{:S(2)}, u32[]{:S(2)}) async-start(bf16[9984,2,96]{2,1,0:T(2,128)(2,1)} %copy.16), calls=%async_computation | async-start | bytes 10223616 | tf_op jit(solution)/shard_map/all_to_all | solution.py:21
  29.2 1059.0 %reduce-scatter.4.cloned.1.call-start = ((), (), s32[]{:S(2)}) async-start(), calls=%async_computation.2 | async-start | bytes 63897600
  164.8 16.9 %copy-start = (bf16[8,1248,2,96]{1,3,0,2:T(8,128)(2,1)S(1)}, bf16[8,1248,2,96]{1,3,0,2:T(8,128)(2,1)}, u32[]{:S(2)}) copy-start(bf16[8,1248,2,96]{1,3,0,2:T(8,128)(2,1)} %copy.18) | copy-start | bytes 11501572
  189.0 43.4 %collective-permute-start = (bf16[1248,1536]{1,0:T(8,128)(2,1)}, bf16[1248,1536]{1,0:T(8,128)(2,1)}, u32[]{:S(2)}, u32[]{:S(2)}) collective-permute-start(bf16[1248,1536]{1,0:T(8,128)(2,1)} %get-tuple-element.210), channel_id=1, source_target_pairs={{1,0},{2,1},{3,2},{4,3},{5,4},{6,5},{7,6},{0,7},{9,8},{10,9},{11,1... | collective-permute-start | bytes 11501576 | tf_op jit(solution)/shard_map/while/body/eval_jaxpr/ppermute | solution.py:10
  189.9 46.7 %copy-start.1 = (bf16[1248,1536]{1,0:T(8,128)(2,1)S(1)}, bf16[1248,1536]{1,0:T(8,128)(2,1)}, u32[]{:S(2)}) copy-start(bf16[1248,1536]{1,0:T(8,128)(2,1)} %get-tuple-element.221) | copy-start | bytes 11501572 | tf_op jit(solution)/shard_map/while
  245.7 46.1 %collective-permute-start = (bf16[1248,1536]{1,0:T(8,128)(2,1)}, bf16[1248,1536]{1,0:T(8,128)(2,1)}, u32[]{:S(2)}, u32[]{:S(2)}) collective-permute-start(bf16[1248,1536]{1,0:T(8,128)(2,1)} %get-tuple-element.210), channel_id=1, source_target_pairs={{1,0},{2,1},{3,2},{4,3},{5,4},{6,5},{7,6},{0,7},{9,8},{10,9},{11,1... | collective-permute-start | bytes 11501576 | tf_op jit(solution)/shard_map/while/body/eval_jaxpr/ppermute | solution.py:10
  249.4 46.7 %copy-start.1 = (bf16[1248,1536]{1,0:T(8,128)(2,1)S(1)}, bf16[1248,1536]{1,0:T(8,128)(2,1)}, u32[]{:S(2)}) copy-start(bf16[1248,1536]{1,0:T(8,128)(2,1)} %get-tuple-element.221) | copy-start | bytes 11501572 | tf_op jit(solution)/shard_map/while
  305.2 46.2 %collective-permute-start = (bf16[1248,1536]{1,0:T(8,128)(2,1)}, bf16[1248,1536]{1,0:T(8,128)(2,1)}, u32[]{:S(2)}, u32[]{:S(2)}) collective-permute-start(bf16[1248,1536]{1,0:T(8,128)(2,1)} %get-tuple-element.210), channel_id=1, source_target_pairs={{1,0},{2,1},{3,2},{4,3},{5,4},{6,5},{7,6},{0,7},{9,8},{10,9},{11,1... | collective-permute-start | bytes 11501576 | tf_op jit(solution)/shard_map/while/body/eval_jaxpr/ppermute | solution.py:10
  308.9 46.7 %copy-start.1 = (bf16[1248,1536]{1,0:T(8,128)(2,1)S(1)}, bf16[1248,1536]{1,0:T(8,128)(2,1)}, u32[]{:S(2)}) copy-start(bf16[1248,1536]{1,0:T(8,128)(2,1)} %get-tuple-element.221) | copy-start | bytes 11501572 | tf_op jit(solution)/shard_map/while
  364.8 46.1 %collective-permute-start = (bf16[1248,1536]{1,0:T(8,128)(2,1)}, bf16[1248,1536]{1,0:T(8,128)(2,1)}, u32[]{:S(2)}, u32[]{:S(2)}) collective-permute-start(bf16[1248,1536]{1,0:T(8,128)(2,1)} %get-tuple-element.210), channel_id=1, source_target_pairs={{1,0},{2,1},{3,2},{4,3},{5,4},{6,5},{7,6},{0,7},{9,8},{10,9},{11,1... | collective-permute-start | bytes 11501576 | tf_op jit(solution)/shard_map/while/body/eval_jaxpr/ppermute | solution.py:10
  368.4 46.7 %copy-start.1 = (bf16[1248,1536]{1,0:T(8,128)(2,1)S(1)}, bf16[1248,1536]{1,0:T(8,128)(2,1)}, u32[]{:S(2)}) copy-start(bf16[1248,1536]{1,0:T(8,128)(2,1)} %get-tuple-element.221) | copy-start | bytes 11501572 | tf_op jit(solution)/shard_map/while
  424.3 46.2 %collective-permute-start = (bf16[1248,1536]{1,0:T(8,128)(2,1)}, bf16[1248,1536]{1,0:T(8,128)(2,1)}, u32[]{:S(2)}, u32[]{:S(2)}) collective-permute-start(bf16[1248,1536]{1,0:T(8,128)(2,1)} %get-tuple-element.210), channel_id=1, source_target_pairs={{1,0},{2,1},{3,2},{4,3},{5,4},{6,5},{7,6},{0,7},{9,8},{10,9},{11,1... | collective-permute-start | bytes 11501576 | tf_op jit(solution)/shard_map/while/body/eval_jaxpr/ppermute | solution.py:10
  428.0 46.7 %copy-start.1 = (bf16[1248,1536]{1,0:T(8,128)(2,1)S(1)}, bf16[1248,1536]{1,0:T(8,128)(2,1)}, u32[]{:S(2)}) copy-start(bf16[1248,1536]{1,0:T(8,128)(2,1)} %get-tuple-element.221) | copy-start | bytes 11501572 | tf_op jit(solution)/shard_map/while
  483.9 46.1 %collective-permute-start = (bf16[1248,1536]{1,0:T(8,128)(2,1)}, bf16[1248,1536]{1,0:T(8,128)(2,1)}, u32[]{:S(2)}, u32[]{:S(2)}) collective-permute-start(bf16[1248,1536]{1,0:T(8,128)(2,1)} %get-tuple-element.210), channel_id=1, source_target_pairs={{1,0},{2,1},{3,2},{4,3},{5,4},{6,5},{7,6},{0,7},{9,8},{10,9},{11,1... | collective-permute-start | bytes 11501576 | tf_op jit(solution)/shard_map/while/body/eval_jaxpr/ppermute | solution.py:10
  487.5 46.7 %copy-start.1 = (bf16[1248,1536]{1,0:T(8,128)(2,1)S(1)}, bf16[1248,1536]{1,0:T(8,128)(2,1)}, u32[]{:S(2)}) copy-start(bf16[1248,1536]{1,0:T(8,128)(2,1)} %get-tuple-element.221) | copy-start | bytes 11501572 | tf_op jit(solution)/shard_map/while
  543.3 46.3 %collective-permute-start = (bf16[1248,1536]{1,0:T(8,128)(2,1)}, bf16[1248,1536]{1,0:T(8,128)(2,1)}, u32[]{:S(2)}, u32[]{:S(2)}) collective-permute-start(bf16[1248,1536]{1,0:T(8,128)(2,1)} %get-tuple-element.210), channel_id=1, source_target_pairs={{1,0},{2,1},{3,2},{4,3},{5,4},{6,5},{7,6},{0,7},{9,8},{10,9},{11,1... | collective-permute-start | bytes 11501576 | tf_op jit(solution)/shard_map/while/body/eval_jaxpr/ppermute | solution.py:10
  547.1 46.7 %copy-start.1 = (bf16[1248,1536]{1,0:T(8,128)(2,1)S(1)}, bf16[1248,1536]{1,0:T(8,128)(2,1)}, u32[]{:S(2)}) copy-start(bf16[1248,1536]{1,0:T(8,128)(2,1)} %get-tuple-element.221) | copy-start | bytes 11501572 | tf_op jit(solution)/shard_map/while
Sparse Core Ops, SparseCore 0:
  656.4 431.6 reduce-scatter.3
where the time goes:
time: 1110 us
  waiting for transfers between devices  843 us (76%)
  local copies, waits for them, and re-layouts  148 us (13%)
  matrix products  71.2 us (6%)
  starting transfers between devices  28.1 us (3%)
  between operations  13.4 us (1%)
    unnamed x2, waiting for transfers between devices  432 us
    ppermute x7, waiting for transfers between devices, shifted(): return lax.ppermute(block, axis, route)  297 us
    all_to_all x1, waiting for transfers between devices, shards(): lax.all_to_all(masked, 'row', split_axis=0, concat_axis=2, tiled=True)  114 us
    unnamed x5, local copies, waits for them, and re-layouts  71.3 us
    dot_general x8, matrix products, tile_with(): lax.dot_general(own_rows, visitor, (((1,), (1,)), ((), ())), preferred_el...  71.2 us
    while x21, local copies, waits for them, and re-layouts  29.5 us
    ppermute x7, starting transfers between devices, shifted(): return lax.ppermute(block, axis, route)  23.1 us
  transfers between devices with their start and end apart: 9, of which 9 were waited for; matrix products, arithmetic and copies ran while one was open for 0% of the time, Pallas kernels for 0%

commit v1 on v0

v1 whole, which is shorter than its diff:
```python
import jax
import jax.numpy as jnp
from jax import lax
from jax.experimental import pallas as pl
from jax.experimental.layout import Layout, with_layout_constraint
from jax.experimental.pallas import tpu as pltpu
from jax.sharding import PartitionSpec as P

LAG = 4


def masked_depth(b_tensor, aux_counts):
    group_index = lax.axis_index("grp")
    slot_count = b_tensor.shape[1]
    live_count = lax.dynamic_index_in_dim(aux_counts, group_index, 0, keepdims=False)
    live_mask = (jnp.arange(slot_count) < live_count).astype(jnp.bfloat16)
    return (b_tensor * live_mask[None, :, None]).reshape(b_tensor.shape[0], -1)


def product(rows, cols):
    return lax.dot_general(
        rows, cols, (((1,), (1,)), ((), ())), preferred_element_type=jnp.float32
    )


def general_shards(b_tensor, aux_counts):
    masked = masked_depth(b_tensor, aux_counts)
    depth = masked.shape[1]
    cols = lax.all_to_all(masked, "grp", split_axis=0, concat_axis=1, tiled=True)
    cols = lax.all_gather(cols, "row", axis=1, tiled=True)
    rows = lax.all_to_all(masked, "row", split_axis=0, concat_axis=1, tiled=True)
    rows = rows.reshape(rows.shape[0], -1, depth)
    rows = lax.all_gather(rows, "grp", axis=2, tiled=True)
    return product(rows.reshape(rows.shape[0], -1), cols)


def gather_kernel(own, cols, rows, own_sem, a_send, u_recv, right_send, left_send,
                  core_send, core_recv, hop_send, hop_recv):
    groups, block, depth = own.shape
    g = lax.axis_index("grp")
    r = lax.axis_index("row")
    z, c = r // 2, r % 2
    gy, gx = g // 2, g % 2
    sy, sx = z // 2, z % 2
    side_y, side_x = (gy + sy) % 2, (gx + sx) % 2
    partner = z * 2 + 1 - c

    def flipped(y, x, m):
        return (y + m // 2) % 2 * 2 + (x + m) % 2

    def at(chunk):
        return pl.ds(pl.multiple_of(chunk * depth, depth), depth)

    mine = pl.ds(pl.multiple_of(c * block, block), block)
    theirs = pl.ds(pl.multiple_of((1 - c) * block, block), block)

    def remote(src, dst, send, recv, grp, row):
        return pltpu.make_async_remote_copy(
            src_ref=src, dst_ref=dst, send_sem=send, recv_sem=recv,
            device_id={"grp": grp, "row": row}, device_id_type=pl.DeviceIdType.MESH)

    barrier = pltpu.get_barrier_semaphore()

    def greet(grp, row):
        pl.semaphore_signal(barrier, inc=1, device_id={"grp": grp, "row": row},
                            device_id_type=pl.DeviceIdType.MESH)

    greet(g, partner)
    for m in range(1, groups):
        greet(flipped(gy, gx, m), r)

    @pl.when(z > 0)
    def _():
        greet(g, r - 2)

    @pl.when(z < groups - 1)
    def _():
        greet(g, r + 2)

    inner = (z > 0).astype(jnp.int32) + (z < groups - 1).astype(jnp.int32)
    pl.semaphore_wait(barrier, groups + inner)

    here = z * groups + g

    def to_group(m):
        peer = flipped(gy, gx, m)
        return remote(own.at[peer], cols.at[mine, at(here)], a_send.at[m],
                      u_recv.at[here], peer, r)

    keep_own = pltpu.make_async_copy(own.at[g], cols.at[mine, at(here)], own_sem)
    keep_own.start()
    for m in range(1, groups):
        to_group(m).start()

    def right(q):
        return remote(cols.at[mine, at(q)], cols.at[mine, at(q)], right_send.at[q],
                      u_recv.at[q], g, r + 2)

    def left(q):
        return remote(cols.at[mine, at(q)], cols.at[mine, at(q)], left_send.at[q],
                      u_recv.at[q], g, r - 2)

    def core(q):
        return remote(cols.at[mine, at(q)], cols.at[mine, at(q)], core_send.at[q],
                      core_recv.at[q], g, partner)

    def hop(src, q, m):
        return remote(src, rows.at[:, at(q)], hop_send.at[q], hop_recv.at[q],
                      flipped(gy, gx, m), r)

    is_source = side_y + side_x == 0

    def step_of(t):
        k, m, side = t // 8, t % 8 // 2, t % 2
        zs = z + (2 * side - 1) * k
        valid = ((k > 0) | (side == 0)) & (zs >= 0) & (zs < groups)
        return k, m, zs, valid

    def hop_mask(m):
        odd = m % 2
        near = (1 - odd) * side_x + odd * side_y
        far = (1 - odd) * side_y + odd * side_x
        last = (near == 0) & (far == 1)
        first_mask = 1 + odd
        second_mask = 2 - odd
        turn = near * (1 - far)
        return turn * second_mask + (1 - turn) * first_mask, last

    steps = groups * groups * 2

    def pass_on(late, place):
        k, m, zs, valid = step_of(jnp.maximum(late, 0))
        mask, last = hop_mask(m)
        near = (1 - m % 2) * side_x + m % 2 * side_y
        here_now = (near == 1) & (side_x + side_y == place)

        @pl.when((late >= 0) & valid & here_now)
        def _():
            q = zs * groups + flipped(sy, sx, m)
            forward = hop(rows.at[:, at(q)], q, mask)
            forward.wait_recv()
            forward.start()

    def advance(t, carry):
        k, m, zs, valid = step_of(t)

        @pl.when((t < steps) & valid)
        def _():
            q = zs * groups + flipped(gy, gx, m)
            is_own = (k == 0) & (m == 0)

            @pl.when(is_own)
            def _():
                keep_own.wait()

            @pl.when(jnp.logical_not(is_own))
            def _():
                core_like = remote(cols.at[mine, at(q)], cols.at[mine, at(q)],
                                   core_send.at[q], u_recv.at[q], g, partner)
                core_like.wait_recv()

            @pl.when((zs <= z) & (z < groups - 1))
            def _():
                right(q).start()

            @pl.when((zs >= z) & (z > 0))
            def _():
                left(q).start()

            core(q).start()

            @pl.when(is_source)
            def _():
                hop(cols.at[mine, at(q)], q, hop_mask(m)[0]).start()

        for place in (1, 2):
            pass_on(t - LAG * place, place)

        return carry

    lax.fori_loop(0, steps + 2 * LAG, advance, 0)

    for m in range(1, groups):
        to_group(m).wait_send()

    def drain(q, carry):
        zs, gs = q // groups, q % groups

        @pl.when((zs <= z) & (z < groups - 1))
        def _():
            right(q).wait_send()

        @pl.when((zs >= z) & (z > 0))
        def _():
            left(q).wait_send()

        core(q).wait_send()
        remote(cols.at[theirs, at(q)], cols.at[theirs, at(q)], core_send.at[q],
               core_recv.at[q], g, partner).wait_recv()
        odd = (gs % 2 + sx) % 2
        mask, last = hop_mask(odd)

        @pl.when(jnp.logical_not(last))
        def _():
            hop(rows.at[:, at(q)], q, mask).wait_send()

        @pl.when(last)
        def _():
            hop(rows.at[:, at(q)], q, mask).wait_recv()

        return carry

    lax.fori_loop(0, groups * groups, drain, 0)


def square_shards(b_tensor, aux_counts):
    groups = lax.axis_size("grp")
    row_count = lax.axis_size("row")
    masked = masked_depth(b_tensor, aux_counts)
    masked = with_layout_constraint(masked, Layout(major_to_minor=(0, 1)))
    depth = masked.shape[1]
    c = lax.axis_index("row") % 2
    halves = masked.reshape(groups, 2, -1, depth)
    mine = lax.dynamic_index_in_dim(halves, c, 1, keepdims=False)
    other = lax.dynamic_index_in_dim(halves, 1 - c, 1, keepdims=False)
    swap = [(i, i + 1 - 2 * (i % 2)) for i in range(row_count)]
    got = lax.ppermute(other, "row", swap)
    own = jnp.concatenate(
        [jnp.where(c == 0, mine, got), jnp.where(c == 0, got, mine)], axis=2
    )
    block = own.shape[1]
    chunks = groups * groups
    dma = pltpu.SemaphoreType.DMA
    anywhere = pl.BlockSpec(memory_space=pl.ANY)
    cols, rows = pl.pallas_call(
        gather_kernel,
        out_shape=[
            jax.ShapeDtypeStruct((2 * block, chunks * 2 * depth), jnp.bfloat16),
            jax.ShapeDtypeStruct((block, chunks * 2 * depth), jnp.bfloat16),
        ],
        in_specs=[anywhere],
        out_specs=[anywhere, anywhere],
        scratch_shapes=[dma, dma((groups,))] + [dma((chunks,))] * 7,
        compiler_params=pltpu.CompilerParams(collective_id=0, has_side_effects=True),
    )(own)
    place = jnp.where(lax.axis_index("row") // 2 == lax.axis_index("grp"), 1 + c, 0)
    return lax.switch(
        place,
        [
            lambda rows, cols: product(rows, cols),
            lambda rows, cols: product(cols[:block], cols),
            lambda rows, cols: product(cols[block:], cols),
        ],
        rows,
        cols,
    )


def solution(mesh):
    groups, row_count = mesh.shape["grp"], mesh.shape["row"]
    square = groups == 4 and row_count == 2 * groups
    return jax.shard_map(
        square_shards if square else general_shards,
        mesh=mesh,
        in_specs=(P(None, "grp", "row"), P()),
        out_specs=P("row", "grp"),
        check_vma=False,
    )
```

time: 1110 us -> 426 us (0.38)
  waiting for transfers between devices: 843 us -> 4.31 us
  Pallas kernels: 0 us -> 346 us
  local copies, waits for them, and re-layouts: 148 us -> 14.8 us
  starting transfers between devices: 28.1 us -> 0.01 us
  matrix products: 71.2 us -> 49.5 us
  between operations: 13.4 us -> 0.03 us
    unnamed x2 -> x0, waiting for transfers between devices: 432 us -> none
    pallas_call x0 -> x1, Pallas kernels: none -> 346 us  [square_shards(): pl.pallas_call(gather_kernel, out_shape=[jax.ShapeDtypeStruct((2 * block,...]
    ppermute x7 -> x1, waiting for transfers between devices: 297 us -> 4.31 us  [square_shards(): got = lax.ppermute(other, 'row', swap)]
    all_to_all x1 -> x0, waiting for transfers between devices: 114 us -> none  [shards(): lax.all_to_all(masked, 'row', split_axis=0, concat_axis=2, tiled=True)]
    unnamed x5 -> x0, local copies, waits for them, and re-layouts: 71.3 us -> none
    while x22 -> x0, local copies, waits for them, and re-layouts: 35.7 us -> none
    ppermute x7 -> x1, starting transfers between devices: 23.1 us -> 0.01 us  [square_shards(): got = lax.ppermute(other, 'row', swap)]
    dot_general x8 -> x1, matrix products: 71.2 us -> 49.5 us  [product(): lax.dot_general(rows, cols, (((1,), (1,)), ((), ())), preferred_element_t...]
  transfers between devices with their start and end apart: 9 -> 1, of which waited for: 9 -> 1; matrix products, arithmetic and copies ran while one was open for 0% -> 0% of each run, Pallas kernels for 0% -> 0%
where the time goes in v1:
time: 426 us; the launch traced here: 425 us
  Pallas kernels  346 us (81%)
  matrix products  49.5 us (12%)
  local copies, waits for them, and re-layouts  14.8 us (3%)
  other arithmetic  10.2 us (2%)
  waiting for transfers between devices  4.31 us (1%)
    pallas_call x1, Pallas kernels, square_shards(): pl.pallas_call(gather_kernel, out_shape=[jax.ShapeDtypeStruct((2 * block,...  346 us
    dot_general x1, matrix products, product(): lax.dot_general(rows, cols, (((1,), (1,)), ((), ())), preferred_element_t...  49.5 us
  transfers between devices with their start and end apart: 1, of which 1 were waited for; matrix products, arithmetic and copies ran while one was open for 0% of the time, Pallas kernels for 0%

profile of v1, /device:TPU:2, one launch (start us, length us, event | category | flops | bytes accessed | tf_op | source)
XLA Modules:
  0.0 425.3 jit_solution(15803363339683219368)
XLA Ops:
  0.0 1.2 dynamic_slice.11
  1.2 0.6 compare_convert_fusion
  1.9 4.3 %broadcast_multiply_fusion = bf16[9984,2,96]{0,2,1:T(8,128)(2,1)} fusion(bf16[9984,2,96]{0,2,1:T(8,128)(2,1)} %param.5, bf16[2]{0:T(256)(128)(2,1)S(1)} %compare_convert_fusion), kind=kLoop, calls=%fused_computation.7 | loop fusion | flops 1916928 | bytes 7667716 | tf_op jit(solution)/shard_map/mul | solution.py:17
  6.2 6.5 %copy.12 = bf16[9984,192]{1,0:T(8,128)(2,1)} copy(bf16[9984,192]{0,1:T(8,128)(2,1)} %bitcast.15) | data formatting | bytes 7667712 | tf_op jit(solution)/shard_map/reshape | solution.py:17
  12.6 1.9 constant_dynamic-slice_fusion
  14.5 2.4 copy.14
  16.9 0.0 collective-permute-start
  16.9 4.3 %collective-permute-done = bf16[4,1248,192]{1,2,0:T(8,128)(2,1)} collective-permute-done((bf16[4,1248,192]{1,2,0:T(8,128)(2,1)}, bf16[4,1248,192]{1,2,0:T(8,128)(2,1)}, u32[]{:S(2)}, u32[]{:S(2)}) %collective-permute-start) | collective-permute-done | bytes 1916960 | tf_op jit(solution)/shard_map/ppermute | solution.py:227
  21.2 2.8 copy.15
  24.1 2.1 bitcast_select_fusion.1
  26.1 3.2 pad_maximum_fusion.own
  29.4 346.4 %shard_map.31 = (bf16[2496,6144]{1,0:T(8,128)(2,1)}, bf16[1248,6144]{1,0:T(8,128)(2,1)}) custom-call(bf16[4,1248,384]{2,1,0:T(8,128)(2,1)} %pad_maximum_fusion.own), custom_call_target="tpu_custom_call" | custom-call | tf_op jit(solution)/shard_map/pallas_call | solution.py:235
  375.8 49.5 %conditional.1 = (f32[1248,2496]{1,0:T(8,128)}) conditional(s32[]{:T(128)} %clamp.3, (bf16[1248,6144]{1,0:T(8,128)(2,1)}, bf16[2496,6144]{1,0:T(8,128)(2,1)}) %tuple.14, bf16[2496,6144]{1,0:T(8,128)(2,1)} %get-tuple-element.20, bf16[2496,6144]{1,0:T(8,128)(2,1)} %get-tuple-element.20), branch_computations={%region_0.1_spmd, %region_1.2_spmd, %region_2.3_spmd} | conditional | flops 38277218304 | bytes 58466312 | solution.py:247
  375.8 49.5 %fusion.4 = f32[1248,2496]{1,0:T(8,128)} fusion(bf16[1248,6144]{1,0:T(8,128)(2,1)} %get-tuple-element.15, bf16[2496,6144]{1,0:T(8,128)(2,1)} %get-tuple-element.16), kind=kOutput, calls=%fused_computation.10 | convolution fusion | flops 38277218304 | bytes 58466304 | tf_op jit(solution)/shard_map/cond/branch_0_fun/dot_general | solution.py:21
Async XLA Ops:
  16.9 4.3 %collective-permute-start = (bf16[4,1248,192]{1,2,0:T(8,128)(2,1)}, bf16[4,1248,192]{1,2,0:T(8,128)(2,1)}, u32[]{:S(2)}, u32[]{:S(2)}) collective-permute-start(bf16[4,1248,192]{1,2,0:T(8,128)(2,1)} %bitcast.16), channel_id=1, source_target_pairs={{0,1},{1,0},{2,3},{3,2},{4,5},{5,4},{6,7},{7,6},{8,9},{9,8},{10,11... | collective-permute-start | bytes 5750792 | tf_op jit(solution)/shard_map/ppermute | solution.py:227

commit v2 on v1

--- a/solution.py
+++ b/solution.py
@@ -92,16 +92,19 @@
     for m in range(1, groups):
         to_group(m).start()
 
-    def right(q):
-        return remote(cols.at[mine, at(q)], cols.at[mine, at(q)], right_send.at[q],
+    def right(q, src=None):
+        src = cols.at[mine, at(q)] if src is None else src
+        return remote(src, cols.at[mine, at(q)], right_send.at[q],
                       u_recv.at[q], g, r + 2)
 
-    def left(q):
-        return remote(cols.at[mine, at(q)], cols.at[mine, at(q)], left_send.at[q],
+    def left(q, src=None):
+        src = cols.at[mine, at(q)] if src is None else src
+        return remote(src, cols.at[mine, at(q)], left_send.at[q],
                       u_recv.at[q], g, r - 2)
 
-    def core(q):
-        return remote(cols.at[mine, at(q)], cols.at[mine, at(q)], core_send.at[q],
+    def core(q, src=None):
+        src = cols.at[mine, at(q)] if src is None else src
+        return remote(src, cols.at[mine, at(q)], core_send.at[q],
                       core_recv.at[q], g, partner)
 
     def hop(src, q, m):
@@ -141,6 +144,21 @@
             forward.wait_recv()
             forward.start()
 
+    def send_on(src, q, zs, m):
+        @pl.when((zs <= z) & (z < groups - 1))
+        def _():
+            right(q, src).start()
+
+        @pl.when((zs >= z) & (z > 0))
+        def _():
+            left(q, src).start()
+
+        core(q, src).start()
+
+        @pl.when(is_source)
+        def _():
+            hop(src, q, hop_mask(m)[0]).start()
+
     def advance(t, carry):
         k, m, zs, valid = step_of(t)
 
@@ -151,27 +169,13 @@
 
             @pl.when(is_own)
             def _():
-                keep_own.wait()
+                send_on(own.at[g], q, zs, m)
 
             @pl.when(jnp.logical_not(is_own))
             def _():
-                core_like = remote(cols.at[mine, at(q)], cols.at[mine, at(q)],
-                                   core_send.at[q], u_recv.at[q], g, partner)
-                core_like.wait_recv()
-
-            @pl.when((zs <= z) & (z < groups - 1))
-            def _():
-                right(q).start()
-
-            @pl.when((zs >= z) & (z > 0))
-            def _():
-                left(q).start()
-
-            core(q).start()
-
-            @pl.when(is_source)
-            def _():
-                hop(cols.at[mine, at(q)], q, hop_mask(m)[0]).start()
+                held = cols.at[mine, at(q)]
+                remote(held, held, core_send.at[q], u_recv.at[q], g, partner).wait_recv()
+                send_on(held, q, zs, m)
 
         for place in (1, 2):
             pass_on(t - LAG * place, place)
@@ -182,6 +186,8 @@
 
     for m in range(1, groups):
         to_group(m).wait_send()
+
+    keep_own.wait()
 
     def drain(q, carry):
         zs, gs = q // groups, q % groups

time: 426 us -> 394 us (0.925)
  Pallas kernels: 346 us -> 315 us
    pallas_call x1, Pallas kernels: 346 us -> 315 us  [square_shards(): pl.pallas_call(gather_kernel, out_shape=[jax.ShapeDtypeStruct((2 * block,...]
where the time goes in v2:
time: 394 us
  Pallas kernels  315 us (80%)
  matrix products  49.5 us (13%)
  local copies, waits for them, and re-layouts  14.8 us (4%)
  other arithmetic  10.2 us (3%)
  waiting for transfers between devices  4.31 us (1%)
    pallas_call x1, Pallas kernels, square_shards(): pl.pallas_call(gather_kernel, out_shape=[jax.ShapeDtypeStruct((2 * block,...  315 us
    dot_general x1, matrix products, product(): lax.dot_general(rows, cols, (((1,), (1,)), ((), ())), preferred_element_t...  49.5 us
  transfers between devices with their start and end apart: 1, of which 1 were waited for; matrix products, arithmetic and copies ran while one was open for 0% of the time, Pallas kernels for 0%

profile of v2, /device:TPU:2, one launch (start us, length us, event | category | flops | bytes accessed | tf_op | source)
XLA Modules:
  0.0 393.8 jit_solution(8450581372775118455)
XLA Ops:
  0.0 1.2 dynamic_slice.11
  1.2 0.6 compare_convert_fusion
  1.9 4.3 %broadcast_multiply_fusion = bf16[9984,2,96]{0,2,1:T(8,128)(2,1)} fusion(bf16[9984,2,96]{0,2,1:T(8,128)(2,1)} %param.5, bf16[2]{0:T(256)(128)(2,1)S(1)} %compare_convert_fusion), kind=kLoop, calls=%fused_computation.7 | loop fusion | flops 1916928 | bytes 7667716 | tf_op jit(solution)/shard_map/mul | solution.py:17
  6.2 6.5 %copy.12 = bf16[9984,192]{1,0:T(8,128)(2,1)} copy(bf16[9984,192]{0,1:T(8,128)(2,1)} %bitcast.15) | data formatting | bytes 7667712 | tf_op jit(solution)/shard_map/reshape | solution.py:17
  12.6 1.9 constant_dynamic-slice_fusion
  14.5 2.4 copy.14
  16.9 0.0 collective-permute-start
  16.9 4.3 %collective-permute-done = bf16[4,1248,192]{1,2,0:T(8,128)(2,1)} collective-permute-done((bf16[4,1248,192]{1,2,0:T(8,128)(2,1)}, bf16[4,1248,192]{1,2,0:T(8,128)(2,1)}, u32[]{:S(2)}, u32[]{:S(2)}) %collective-permute-start) | collective-permute-done | bytes 1916960 | tf_op jit(solution)/shard_map/ppermute | solution.py:233
  21.2 2.8 copy.15
  24.1 2.1 bitcast_select_fusion.1
  26.1 3.2 pad_maximum_fusion.own
  29.4 314.9 %shard_map.31 = (bf16[2496,6144]{1,0:T(8,128)(2,1)}, bf16[1248,6144]{1,0:T(8,128)(2,1)}) custom-call(bf16[4,1248,384]{2,1,0:T(8,128)(2,1)} %pad_maximum_fusion.own), custom_call_target="tpu_custom_call" | custom-call | tf_op jit(solution)/shard_map/pallas_call | solution.py:241
  344.3 49.5 %conditional.1 = (f32[1248,2496]{1,0:T(8,128)}) conditional(s32[]{:T(128)} %clamp.3, (bf16[1248,6144]{1,0:T(8,128)(2,1)}, bf16[2496,6144]{1,0:T(8,128)(2,1)}) %tuple.14, bf16[2496,6144]{1,0:T(8,128)(2,1)} %get-tuple-element.20, bf16[2496,6144]{1,0:T(8,128)(2,1)} %get-tuple-element.20), branch_computations={%region_0.1_spmd, %region_1.2_spmd, %region_2.3_spmd} | conditional | flops 38277218304 | bytes 58466312 | solution.py:253
  344.3 49.5 %fusion.4 = f32[1248,2496]{1,0:T(8,128)} fusion(bf16[1248,6144]{1,0:T(8,128)(2,1)} %get-tuple-element.15, bf16[2496,6144]{1,0:T(8,128)(2,1)} %get-tuple-element.16), kind=kOutput, calls=%fused_computation.10 | convolution fusion | flops 38277218304 | bytes 58466304 | tf_op jit(solution)/shard_map/cond/branch_0_fun/dot_general | solution.py:21
Async XLA Ops:
  16.9 4.3 %collective-permute-start = (bf16[4,1248,192]{1,2,0:T(8,128)(2,1)}, bf16[4,1248,192]{1,2,0:T(8,128)(2,1)}, u32[]{:S(2)}, u32[]{:S(2)}) collective-permute-start(bf16[4,1248,192]{1,2,0:T(8,128)(2,1)} %bitcast.16), channel_id=1, source_target_pairs={{0,1},{1,0},{2,3},{3,2},{4,5},{5,4},{6,7},{7,6},{8,9},{9,8},{10,11... | collective-permute-start | bytes 5750792 | tf_op jit(solution)/shard_map/ppermute | solution.py:233
